TPU v7x, 32 devices: a whole 2x2x4 slice. The times are simulated.
32 devices in a mesh: node: 8 (over z, x), local: 4 (over y, core).
Axes of the slice: x: 2, y: 2, z: 4, core: 2. Of those that a mesh axis runs over, the one named last changes fastest.
Arguments:
- tokens: bfloat16 [512, 7168], P(('node', 'local')), may hold values from -6 to 6
- expert_ids: int32 [512, 2], P(('node', 'local')), may hold values from 0 to 7, all different within a row; in each aligned block of 16 rows (0 to 15, 16 to 31, ...) at most 4 rows name the same one
- combine_weights: float32 [512, 2], P(('node', 'local')), may hold values from 0.25 to 1
- w_gate: bfloat16 [8, 7168, 1024], P('node', None, 'local'), may hold values from -0.0625 to 0.0625
- w_up: bfloat16 [8, 7168, 1024], P('node', None, 'local'), may hold values from -0.0625 to 0.0625
- w_down: bfloat16 [8, 1024, 7168], P('node', 'local'), may hold values from -0.1875 to 0.1875
Outputs:
- moe_out: bfloat16 [512, 7168], P(('node', 'local'))
Inputs may be any that keep to these rules, and one draw needn't show every extreme that they name: `expert_ids`: each row names 2 different experts. Among the 16 rows of one device no expert is named more than 4 times, and in every draw some expert is named exactly 4 times by the rows of some device.
All inputs are finite; a program needn't handle non-finite values.
Results may differ from a plain program's by a relative error of at most 0.0095.
Values may be sent and summed in bfloat16 or wider, within the bound.
A program may use at most 64 MiB of HBM per device.

v0:
```python
import jax
import jax.numpy as jnp
from jax import lax
from jax.sharding import PartitionSpec as P

CAP = 4


def body(tokens, expert_ids, combine_weights, w_gate, w_up, w_down):
    tok_rows = tokens.shape[0]
    choose = expert_ids.shape[1]
    width = tokens.shape[1]
    node_count = lax.axis_size("node")
    group_size = lax.axis_size("local")
    slots = CAP
    flat_ids = expert_ids.reshape(-1)
    onehot = (flat_ids[:, None] == jnp.arange(node_count, dtype=jnp.int32)[None, :]).astype(
        jnp.int32
    )
    before = jnp.cumsum(onehot, axis=0) - onehot
    slot_of = jnp.sum(before * onehot, axis=1)
    target = flat_ids * slots + slot_of
    positions = jnp.arange(node_count * slots, dtype=jnp.int32)
    selector = jnp.any(
        target.reshape(tok_rows, choose)[None, :, :] == positions[:, None, None], axis=2
    )
    outgoing = jnp.dot(
        selector.astype(jnp.bfloat16), tokens, preferred_element_type=jnp.float32
    ).astype(jnp.bfloat16)
    gate_here = w_gate[0]
    up_here = w_up[0]
    down_here = w_down[0]
    units = gate_here.shape[1]
    copies = jnp.broadcast_to(
        outgoing.reshape(node_count, 1, slots, width), (node_count, group_size, slots, width)
    )
    copies = copies.reshape(node_count * group_size * slots, width)
    arrived = lax.all_to_all(copies, ("node", "local"), split_axis=0, concat_axis=0, tiled=True)
    gated = jnp.dot(arrived, gate_here, preferred_element_type=jnp.float32)
    upward = jnp.dot(arrived, up_here, preferred_element_type=jnp.float32)
    hidden = (
        (jax.nn.silu(gated) * upward)
        .astype(jnp.bfloat16)
        .reshape(node_count, group_size, slots, units)
    )
    hidden = jnp.transpose(hidden, (1, 0, 2, 3)).reshape(group_size * node_count * slots, units)
    ordered = jnp.transpose(hidden.reshape(group_size, node_count, slots, units), (1, 0, 2, 3))
    ordered = ordered.reshape(node_count * group_size * slots, units)
    partial_value = jnp.dot(ordered, down_here, preferred_element_type=jnp.float32).astype(
        jnp.bfloat16
    )
    returned = lax.all_to_all(
        partial_value, ("node", "local"), split_axis=0, concat_axis=0, tiled=True
    )
    summed = jnp.sum(
        returned.reshape(node_count, group_size, slots, width), axis=1, dtype=jnp.float32
    )
    expert_out = summed.astype(jnp.bfloat16).reshape(node_count * slots, width)
    picked = expert_out[target].astype(jnp.float32).reshape(tok_rows, choose, width)
    mixed = jnp.sum(picked * combine_weights[:, :, None], axis=1)
    return mixed.astype(jnp.bfloat16)


def solution(mesh):
    return jax.shard_map(
        body,
        mesh=mesh,
        in_specs=(
            P(("node", "local"), None),
            P(("node", "local"), None),
            P(("node", "local"), None),
            P("node", None, "local"),
            P("node", None, "local"),
            P("node", "local", None),
        ),
        out_specs=P(("node", "local"), None),
        check_vma=False,
    )
```

profile of v0, /device:TPU:0, one launch (start us, length us, event | category | flops | bytes accessed | tf_op | source)
XLA Modules:
  0.0 120.2 jit_solution(16317764443204595741)
XLA Ops:
  0.0 0.0 copy-start
  0.0 0.8 copy.13
  0.8 0.1 eq.28
  0.9 0.1 fusion.19
  1.0 0.1 reduce_window_sum.11
  1.0 0.2 select_reduce_fusion
  1.2 0.1 reduce_sum.35
  1.3 0.1 copy.15
  1.4 0.1 fusion.20
  1.5 0.0 copy-done
  1.5 0.3 convolution_convert_fusion.1
  1.8 0.2 broadcast_in_dim.4
  2.0 0.5 broadcast_in_dim.5
  2.5 50.3 %all_to_all.21 = bf16[32,4,7168]{2,1,0:T(4,128)(2,1)} all-to-all(bf16[32,4,7168]{2,1,0:T(4,128)(2,1)S(1)} %bitcast.28), channel_id=1, replica_groups=mesh['node'=8,'local'=4] {'node','local'}, dimensions={0} | all-to-all | bytes 3670016 | tf_op jit(solution)/shard_map/all_to_all | solution.py:38
  52.8 2.9 %all_to_all.16 = bf16[128,7168]{1,0:T(8,128)(2,1)S(1)} reshape(bf16[32,4,7168]{2,1,0:T(4,128)(2,1)} %all_to_all.21) | data formatting | bytes 3670016 | tf_op jit(solution)/shard_map/all_to_all | solution.py:38
  55.8 2.7 %fusion.3 = f32[128,256]{1,0:T(8,128)S(1)} fusion(bf16[128,7168]{1,0:T(8,128)(2,1)S(1)} %all_to_all.16, bf16[1,7168,256]{2,1,0:T(8,128)(2,1)} %param.9), kind=kOutput, calls=%fused_computation.6 | convolution fusion | flops 469762048 | bytes 5636096 | tf_op jit(solution)/shard_map/dot_general | solution.py:39
  58.5 6.5 %convolution_convert_fusion = bf16[128,7168]{1,0:T(8,128)(2,1)} fusion(bf16[1,256,7168]{2,1,0:T(8,128)(2,1)} %param.11, bf16[128,7168]{1,0:T(8,128)(2,1)S(1)} %all_to_all.16, bf16[1,7168,256]{2,1,0:T(8,128)(2,1)} %param.10, f32[128,256]{1,0:T(8,128)S(1)} %fusion.3), kind=kOutput, calls=%fused_computation.1 | convolution fusion | flops 940638208 | bytes 11141120 | tf_op jit(solution)/shard_map/dot_general | solution.py:49
  65.0 4.1 %all_to_all.17 = bf16[32,4,7168]{2,1,0:T(4,128)(2,1)} reshape(bf16[128,7168]{1,0:T(8,128)(2,1)} %convolution_convert_fusion) | data formatting | bytes 3670016 | tf_op jit(solution)/shard_map/all_to_all | solution.py:52
  69.1 0.0 copy-start.1
  69.1 3.6 %all-to-all-start.1 = ((bf16[32,4,7168]{2,1,0:T(4,128)(2,1)}), bf16[32,4,7168]{2,1,0:T(4,128)(2,1)S(1)}, u32[]{:S(2)}, u32[]{:S(2)}) async-start(bf16[32,4,7168]{2,1,0:T(4,128)(2,1)} %all_to_all.17), calls=%async_computation.1 | async-start | bytes 3670016 | tf_op jit(solution)/shard_map/all_to_all | solution.py:52
  72.7 0.1 mul.41
  72.8 0.0 copy-done.1
  72.8 0.1 copy.16
  72.9 42.9 %all-to-all-done.1 = bf16[32,4,7168]{2,1,0:T(4,128)(2,1)S(1)} async-done(((bf16[32,4,7168]{2,1,0:T(4,128)(2,1)}), bf16[32,4,7168]{2,1,0:T(4,128)(2,1)S(1)}, u32[]{:S(2)}, u32[]{:S(2)}) %all-to-all-start.1) | async-done | bytes 1835040 | tf_op jit(solution)/shard_map/all_to_all | solution.py:52
  115.8 0.9 bitcast_reduce_fusion
  116.7 0.1 reshape.57
  116.8 0.8 gather_fusion
  117.7 0.6 reshape.58
  118.3 1.9 %multiply_reduce_fusion = bf16[16,7168]{1,0:T(8,128)(2,1)} fusion(f32[16,2,7168]{2,1,0:T(2,128)S(1)} %reshape.58, f32[16,2]{1,0:T(8,128)S(1)} %copy.16), kind=kLoop, calls=%fused_computation.11 | loop fusion | flops 344064 | bytes 1147008 | tf_op jit(solution)/shard_map/reduce_sum | solution.py:60
  (3 shorter events, 0.0 us)
Async XLA Ops:
  0.0 1.5 %copy-start = (bf16[16,7168]{1,0:T(8,128)(2,1)S(1)}, bf16[16,7168]{1,0:T(8,128)(2,1)}, u32[]{:S(2)}) copy-start(bf16[16,7168]{1,0:T(8,128)(2,1)} %param.6) | copy-start | bytes 688132
  69.1 3.7 %copy-start.1 = (f32[16,2]{0,1:T(2,128)S(1)}, f32[16,2]{0,1:T(2,128)}, u32[]{:S(2)}) copy-start(f32[16,2]{0,1:T(2,128)} %param.8) | copy-start | bytes 388
  69.1 46.8 %all-to-all-start.1 = ((bf16[32,4,7168]{2,1,0:T(4,128)(2,1)}), bf16[32,4,7168]{2,1,0:T(4,128)(2,1)S(1)}, u32[]{:S(2)}, u32[]{:S(2)}) async-start(bf16[32,4,7168]{2,1,0:T(4,128)(2,1)} %all_to_all.17), calls=%async_computation.1 | async-start | bytes 3670016 | tf_op jit(solution)/shard_map/all_to_all | solution.py:52
where the time goes:
time: 121 us; the launch traced here: 120 us
  blocking collectives  50.3 us (42%)
  waiting for transfers between devices  42.9 us (35%)
  local copies, waits for them, and re-layouts  10.4 us (9%)
  matrix products  9.56 us (8%)
  starting transfers between devices  3.62 us (3%)
  other arithmetic  3.22 us (3%)
    all_to_all x1, blocking collectives, body(): lax.all_to_all(copies, ('node', 'local'), split_axis=0, concat_axis=0, ti...  50.3 us
    all_to_all x1, waiting for transfers between devices, body(): lax.all_to_all(partial_value, ('node', 'local'), split_axis=0, concat_axi...  42.9 us
    dot_general x1, matrix products, body(): jnp.dot(ordered, down_here, preferred_element_type=jnp.float32)  6.55 us
    all_to_all x1, local copies, waits for them, and re-layouts, body(): lax.all_to_all(partial_value, ('node', 'local'), split_axis=0, concat_axi...  4.06 us
    all_to_all x1, starting transfers between devices, body(): lax.all_to_all(partial_value, ('node', 'local'), split_axis=0, concat_axi...  3.62 us
    all_to_all x1, local copies, waits for them, and re-layouts, body(): lax.all_to_all(copies, ('node', 'local'), split_axis=0, concat_axis=0, ti...  2.94 us
    dot_general x1, matrix products, body(): gated = jnp.dot(arrived, gate_here, preferred_element_type=jnp.float32)  2.69 us
  transfers between devices with their start and end apart: 1, of which 1 were waited for; matrix products, arithmetic and copies ran while one was open for 0% of the time, Pallas kernels for 0%

commit v1 on v0

v1 whole, which is shorter than its diff:
```python
import functools
import jax
import jax.numpy as jnp
from jax import lax
from jax.experimental import pallas as pl
from jax.experimental.pallas import tpu as pltpu
from jax.sharding import PartitionSpec as P

CAP = 4
MESH = pl.DeviceIdType.MESH


def flip(index, mask):
    bit = 1
    total = index
    while bit <= mask:
        if mask & bit:
            total = total + bit * (1 - 2 * lax.rem(index // bit, 2))
        bit *= 2
    return total


def kernel(
    nodes, chips, order, groups,
    tok_ref, ids_ref, wts_ref, gate_hbm, up_hbm, down_hbm, out_ref,
    gate, up, down, outgoing, arrived, hidden, partial, from_core, chip_sum, from_chip, expert_out, back,
    w_sem, s_node, r_node, s_core, r_core, s_chip, r_chip, s_fwd, r_fwd,
    s_core2, r_core2, s_chip2, r_chip2, s_node2, r_node2,
):
    width = tok_ref.shape[1]
    rows = tok_ref.shape[0]
    units = gate.shape[1]
    slots = CAP
    pieces = 4
    step = width // pieces
    columns = [slice(q * step, (q + 1) * step) for q in range(pieces)]
    n = lax.axis_index("node")
    l = lax.axis_index("local")
    y = l // 2
    c = lax.rem(l, 2)
    oc = 1 - c

    loads = [
        pltpu.make_async_copy(src.at[0], dst, w_sem.at[i])
        for i, (src, dst) in enumerate(((gate_hbm, gate), (up_hbm, up), (down_hbm, down)))
    ]
    for load in loads:
        load.start()

    def chip_at(step_y):
        return lax.rem(y + step_y, chips)

    def dev(node, chip, core):
        return (node, chip * 2 + core)

    barrier = pltpu.get_barrier_semaphore()
    peers = [dev(flip(n, k), y, c) for k in order if k]
    peers += [dev(n, y, oc)] + [dev(n, chip_at(d), c) for d in range(1, chips)]
    for peer in peers:
        pl.semaphore_signal(barrier, inc=1, device_id=peer, device_id_type=MESH)

    ids = ids_ref[...]
    wts = wts_ref[...]
    places = nodes * slots
    place = lax.broadcasted_iota(jnp.int32, (rows, places), 1)
    first = ids[:, 0:1] == place // slots
    second = ids[:, 1:2] == place // slots
    named = jnp.where(first | second, 1.0, 0.0)
    lower = jnp.where(
        lax.broadcasted_iota(jnp.int32, (rows, rows), 1)
        < lax.broadcasted_iota(jnp.int32, (rows, rows), 0), 1.0, 0.0,
    )
    rank = jnp.dot(lower, named, preferred_element_type=jnp.float32)
    chosen = jnp.where(rank == lax.rem(place, slots).astype(jnp.float32), named, 0.0)
    weight = chosen * jnp.where(first, wts[:, 0:1], wts[:, 1:2])
    weight_hi = weight.astype(jnp.bfloat16)
    weight_lo = (weight - weight_hi.astype(jnp.float32)).astype(jnp.bfloat16)
    chosen = chosen.astype(jnp.bfloat16)
    for cols in columns:
        sent = lax.dot_general(
            chosen, tok_ref[:, cols], (((0,), (0,)), ((), ())),
            preferred_element_type=jnp.float32,
        )
        outgoing[:, :, cols] = sent.astype(jnp.bfloat16).reshape(nodes, slots, step)
    mine = c * chips + y
    p_own = order.index(0)
    arrived[p_own, c, y] = outgoing[n]

    pl.semaphore_wait(barrier, len(peers))

    def remote(src, dst, s_sem, r_sem, to):
        return pltpu.make_async_remote_copy(
            src_ref=src, dst_ref=dst, send_sem=s_sem, recv_sem=r_sem,
            device_id=to, device_id_type=MESH,
        )

    started = []

    def go(copy):
        copy.start()
        started.append(copy)

    def node_copy(p):
        to = flip(n, order[p])
        return remote(outgoing.at[to], arrived.at[p, c, y], s_node.at[p], r_node.at[p], dev(to, y, c))

    for p in reversed(range(nodes)):
        if p != p_own:
            go(node_copy(p))

    def core_copy(p):
        slab = arrived.at[p, c, y]
        return remote(slab, slab, s_core.at[p], r_core.at[p], dev(n, y, oc))

    def chip_copy(p, d):
        slab = arrived.at[p, c, y]
        return remote(slab, slab, s_chip.at[d - 1, p], r_chip.at[d - 1, p], dev(n, chip_at(d), c))

    def chip_arrival(p, d):
        slab = arrived.at[p, c, chip_at(chips - d)]
        return remote(slab, slab, s_chip.at[d - 1, p], r_chip.at[d - 1, p], dev(n, chip_at(d), c))

    def fwd_copy(p, d):
        slab = arrived.at[p, c, chip_at(chips - d)]
        return remote(slab, slab, s_fwd.at[d - 1, p], r_fwd.at[d - 1, p], dev(n, y, oc))

    def fwd_arrival(p, d):
        slab = arrived.at[p, oc, chip_at(chips - d)]
        return remote(slab, slab, s_fwd.at[d - 1, p], r_fwd.at[d - 1, p], dev(n, y, oc))

    def spread(p):
        if p != p_own:
            node_copy(p).wait_recv()
        for d in range(1, chips):
            go(chip_copy(p, d))
        go(core_copy(p))

    def forward(p):
        for d in range(1, chips):
            chip_arrival(p, d).wait_recv()
            go(fwd_copy(p, d))

    def core_copy2(p):
        return remote(partial.at[p, oc], from_core.at[p], s_core2.at[p], r_core2.at[p], dev(n, y, oc))

    def compute(lo, hi):
        for p in range(lo, hi):
            slab = arrived.at[p, oc, y]
            remote(slab, slab, s_core.at[p], r_core.at[p], dev(n, y, oc)).wait_recv()
            for d in range(1, chips):
                fwd_arrival(p, d).wait_recv()
        count = (hi - lo) * 2 * chips * slots
        gated = jnp.zeros((count, units), jnp.float32)
        upward = jnp.zeros((count, units), jnp.float32)
        if lo == 0:
            loads[0].wait()
            loads[1].wait()
        for cols in columns:
            x = arrived[lo:hi, :, :, :, cols].reshape(count, step)
            gated += jnp.dot(x, gate[cols, :], preferred_element_type=jnp.float32)
            upward += jnp.dot(x, up[cols, :], preferred_element_type=jnp.float32)
        hidden[0:count] = (gated / (1.0 + jnp.exp(-gated)) * upward).astype(jnp.bfloat16)
        if lo == 0:
            loads[2].wait()
        for cols in columns:
            value = jnp.dot(hidden[0:count], down[:, cols], preferred_element_type=jnp.float32)
            partial[lo:hi, :, :, :, cols] = value.astype(jnp.bfloat16).reshape(
                hi - lo, 2, chips, slots, step
            )
        for p in range(lo, hi):
            go(core_copy2(p))

    def chip_copy2(p, d):
        return remote(
            chip_sum.at[p, d - 1], from_chip.at[p, d - 1], s_chip2.at[d - 1, p], r_chip2.at[d - 1, p],
            dev(n, chip_at(d), c),
        )

    def to_chips(p):
        core_copy2(p).wait_recv()
        for d in range(1, chips):
            other = chip_at(d)
            both = partial[p, c, other].astype(jnp.float32) + from_core[p, other].astype(jnp.float32)
            chip_sum[p, d - 1] = both.astype(jnp.bfloat16)
            go(chip_copy2(p, d))

    def node_copy2(p):
        return remote(
            expert_out.at[p], back.at[n], s_node2.at[p], r_node2.at[p], dev(flip(n, order[p]), y, c)
        )

    def to_nodes(p):
        total = partial[p, c, y].astype(jnp.float32) + from_core[p, y].astype(jnp.float32)
        for d in range(1, chips):
            chip_copy2(p, d).wait_recv()
            total += from_chip[p, d - 1].astype(jnp.float32)
        if p == p_own:
            back[n] = total.astype(jnp.bfloat16)
        else:
            expert_out[p] = total.astype(jnp.bfloat16)
            go(node_copy2(p))

    lag = 2
    for p in range(nodes + lag):
        if p < nodes:
            spread(p)
        if p >= lag:
            forward(p - lag)
    bounds = [(i * nodes // groups, (i + 1) * nodes // groups) for i in range(groups)]
    for lo, hi in bounds:
        compute(lo, hi)
        for p in range(lo, hi):
            to_chips(p)
    for p in range(nodes):
        to_nodes(p)
    for p in range(nodes):
        if p != p_own:
            src = flip(n, order[p])
            remote(
                expert_out.at[p], back.at[src], s_node2.at[p], r_node2.at[p], dev(src, y, c)
            ).wait_recv()
    for cols in columns:
        rows_back = back[:, :, cols].reshape(places, step)
        mixed = jnp.dot(weight_hi, rows_back, preferred_element_type=jnp.float32)
        mixed += jnp.dot(weight_lo, rows_back, preferred_element_type=jnp.float32)
        out_ref[:, cols] = mixed.astype(jnp.bfloat16)
    for copy in started:
        copy.wait_send()


def body(nodes, chips, tokens, expert_ids, combine_weights, w_gate, w_up, w_down):
    rows, width = tokens.shape
    units = w_gate.shape[2]
    order = sorted(range(nodes), key=lambda k: (k.bit_count(), k))
    groups = 2
    slab = (CAP, width)
    bf = jnp.bfloat16
    sems = pltpu.SemaphoreType.DMA
    vmem = pl.BlockSpec(memory_space=pltpu.VMEM)
    hbm = pl.BlockSpec(memory_space=pl.ANY)
    return pl.pallas_call(
        functools.partial(kernel, nodes, chips, order, groups),
        out_shape=jax.ShapeDtypeStruct((rows, width), bf),
        in_specs=[vmem, vmem, vmem, hbm, hbm, hbm],
        out_specs=vmem,
        scratch_shapes=[
            pltpu.VMEM((width, units), bf),
            pltpu.VMEM((width, units), bf),
            pltpu.VMEM((units, width), bf),
            pltpu.VMEM((nodes,) + slab, bf),
            pltpu.VMEM((nodes, 2, chips) + slab, bf),
            pltpu.VMEM((nodes * 2 * chips * CAP, units), bf),
            pltpu.VMEM((nodes, 2, chips) + slab, bf),
            pltpu.VMEM((nodes, chips) + slab, bf),
            pltpu.VMEM((nodes, chips - 1) + slab, bf),
            pltpu.VMEM((nodes, chips - 1) + slab, bf),
            pltpu.VMEM((nodes,) + slab, bf),
            pltpu.VMEM((nodes,) + slab, bf),
            sems((3,)),
            sems((nodes,)), sems((nodes,)),
            sems((nodes,)), sems((nodes,)),
            sems((chips - 1, nodes)), sems((chips - 1, nodes)),
            sems((chips - 1, nodes)), sems((chips - 1, nodes)),
            sems((nodes,)), sems((nodes,)),
            sems((chips - 1, nodes)), sems((chips - 1, nodes)),
            sems((nodes,)), sems((nodes,)),
        ],
        compiler_params=pltpu.CompilerParams(
            collective_id=0, has_side_effects=True, vmem_limit_bytes=56 * 1024 * 1024
        ),
        name="routed_experts",
    )(tokens, expert_ids, combine_weights, w_gate, w_up, w_down)


def solution(mesh):
    nodes = mesh.shape["node"]
    chips = mesh.shape["local"] // 2
    return jax.shard_map(
        functools.partial(body, nodes, chips),
        mesh=mesh,
        in_specs=(
            P(("node", "local"), None),
            P(("node", "local"), None),
            P(("node", "local"), None),
            P("node", None, "local"),
            P("node", None, "local"),
            P("node", "local", None),
        ),
        out_specs=P(("node", "local"), None),
        check_vma=False,
    )
```

time: 121 us -> 52.4 us (0.43)
  blocking collectives: 50.3 us -> 0 us
  Pallas kernels: 0 us -> 47.8 us
  waiting for transfers between devices: 42.9 us -> 0 us
  matrix products: 9.56 us -> 0 us
  local copies, waits for them, and re-layouts: 10.4 us -> 4.34 us
  starting transfers between devices: 3.62 us -> 0 us
  other arithmetic: 3.22 us -> 0 us
    all_to_all x1 -> x0, blocking collectives: 50.3 us -> none  [body(): lax.all_to_all(copies, ('node', 'local'), split_axis=0, concat_axis=0, ti...]
    pallas_call x0 -> x1, Pallas kernels: none -> 47.8 us  [body(): pl.pallas_call(functools.partial(kernel, nodes, chips, order, groups), ou...]
    all_to_all x1 -> x0, waiting for transfers between devices: 42.9 us -> none  [body(): lax.all_to_all(partial_value, ('node', 'local'), split_axis=0, concat_axi...]
    dot_general x3 -> x0, matrix products: 9.56 us -> none  [the longest x1 6.55 us: body(): jnp.dot(ordered, down_here, preferred_element_type=jnp.float32)]
    all_to_all x2 -> x0, local copies, waits for them, and re-layouts: 6.99 us -> none  [the longest x1 4.06 us: body(): lax.all_to_all(partial_value, ('node', 'local'), split_axis=0, concat_axi...]
    all_to_all x1 -> x0, starting transfers between devices: 3.62 us -> none  [body(): lax.all_to_all(partial_value, ('node', 'local'), split_axis=0, concat_axi...]
    unnamed x6 -> x3, local copies, waits for them, and re-layouts: 0.89 us -> 4.34 us
    reduce_sum x3 -> x0, other arithmetic: 2.99 us -> none  [the longest x1 1.92 us: body(): mixed = jnp.sum(picked * combine_weights[:, :, None], axis=1)]
  transfers between devices with their start and end apart: 1 -> 0, of which waited for: 1 -> 0; matrix products, arithmetic and copies ran while one was open for 0% -> 0% of each run, Pallas kernels for 0% -> 0%
where the time goes in v1:
time: 52.4 us; the launch traced here: 52.1 us
  Pallas kernels  47.8 us (91%)
  local copies, waits for them, and re-layouts  4.34 us (8%)
    pallas_call x1, Pallas kernels, body(): pl.pallas_call(functools.partial(kernel, nodes, chips, order, groups), ou...  47.8 us
    unnamed x3, local copies, waits for them, and re-layouts  4.34 us

profile of v1, /device:TPU:0, one launch (start us, length us, event | category | flops | bytes accessed | tf_op | source)
XLA Modules:
  0.0 52.1 jit_solution(11320646579364539355)
XLA Ops:
  0.0 1.4 %copy.7.ids_ref = s32[16,2]{1,0:T(8,128)} copy(s32[16,2]{0,1:T(2,128)} %param.7) | data formatting | bytes 256 | tf_op args[1]
  1.4 1.4 %copy.8.wts_ref = f32[16,2]{1,0:T(8,128)} copy(f32[16,2]{0,1:T(2,128)} %param.8) | data formatting | bytes 256 | tf_op args[2]
  2.7 47.8 %routed_experts.1 = bf16[16,7168]{1,0:T(8,128)(2,1)} custom-call(bf16[16,7168]{1,0:T(8,128)(2,1)} %tok_ref.1, s32[16,2]{1,0:T(8,128)} %copy.7.ids_ref, f32[16,2]{1,0:T(8,128)} %copy.8.wts_ref, bf16[1,7168,256]{2,1,0:T(8,128)(2,1)} %gate_hbm.1, bf16[1,7168,256]{2,1,0:T(8,128)(2,1)} %up_hbm.1, bf16[1,256,7168]{2,1,0:T(8,128)(2,1)} %down_hbm.1), custom_call_target="tpu_custom_call" | custom-call | tf_op jit(solution)/shard_map/routed_experts/pallas_call | solution.py:241
  50.5 1.6 %copy.10 = bf16[16,7168]{1,0:T(8,128)(2,1)} copy(bf16[16,7168]{1,0:T(8,128)(2,1)} %routed_experts.1) | data formatting | bytes 458752

commit v2 on v1

--- a/solution.py
+++ b/solution.py
@@ -21,7 +21,7 @@
 
 
 def kernel(
-    nodes, chips, order, groups,
+    nodes, chips, order, early, way_back, groups, windows,
     tok_ref, ids_ref, wts_ref, gate_hbm, up_hbm, down_hbm, out_ref,
     gate, up, down, outgoing, arrived, hidden, partial, from_core, chip_sum, from_chip, expert_out, back,
     w_sem, s_node, r_node, s_core, r_core, s_chip, r_chip, s_fwd, r_fwd,
@@ -55,6 +55,7 @@
 
     barrier = pltpu.get_barrier_semaphore()
     peers = [dev(flip(n, k), y, c) for k in order if k]
+    peers += [dev(flip(n, order[p]), chip_at(d), c) for p in early for d in range(1, chips)]
     peers += [dev(n, y, oc)] + [dev(n, chip_at(d), c) for d in range(1, chips)]
     for peer in peers:
         pl.semaphore_signal(barrier, inc=1, device_id=peer, device_id_type=MESH)
@@ -62,27 +63,23 @@
     ids = ids_ref[...]
     wts = wts_ref[...]
     places = nodes * slots
-    place = lax.broadcasted_iota(jnp.int32, (rows, places), 1)
-    first = ids[:, 0:1] == place // slots
-    second = ids[:, 1:2] == place // slots
+    place = lax.broadcasted_iota(jnp.int32, (places, rows), 0)
+    first = ids[0:1, :] == place // slots
+    second = ids[1:2, :] == place // slots
     named = jnp.where(first | second, 1.0, 0.0)
-    lower = jnp.where(
-        lax.broadcasted_iota(jnp.int32, (rows, rows), 1)
-        < lax.broadcasted_iota(jnp.int32, (rows, rows), 0), 1.0, 0.0,
+    before = jnp.where(
+        lax.broadcasted_iota(jnp.int32, (rows, rows), 0)
+        < lax.broadcasted_iota(jnp.int32, (rows, rows), 1), 1.0, 0.0,
     )
-    rank = jnp.dot(lower, named, preferred_element_type=jnp.float32)
+    rank = jnp.dot(named, before, preferred_element_type=jnp.float32)
     chosen = jnp.where(rank == lax.rem(place, slots).astype(jnp.float32), named, 0.0)
-    weight = chosen * jnp.where(first, wts[:, 0:1], wts[:, 1:2])
+    weight = chosen * jnp.where(first, wts[0:1, :], wts[1:2, :])
     weight_hi = weight.astype(jnp.bfloat16)
     weight_lo = (weight - weight_hi.astype(jnp.float32)).astype(jnp.bfloat16)
     chosen = chosen.astype(jnp.bfloat16)
     for cols in columns:
-        sent = lax.dot_general(
-            chosen, tok_ref[:, cols], (((0,), (0,)), ((), ())),
-            preferred_element_type=jnp.float32,
-        )
+        sent = jnp.dot(chosen, tok_ref[:, cols], preferred_element_type=jnp.float32)
         outgoing[:, :, cols] = sent.astype(jnp.bfloat16).reshape(nodes, slots, step)
-    mine = c * chips + y
     p_own = order.index(0)
     arrived[p_own, c, y] = outgoing[n]
 
@@ -94,19 +91,37 @@
             device_id=to, device_id_type=MESH,
         )
 
-    started = []
-
-    def go(copy):
+    started, node_queue, chip_queue, chip_queue2, node_queue2 = [], [], [], [], []
+    node_window, chip_window, chip_window2, node_window2, lag, lag2 = windows
+
+    def go(copy, queue=None, window=0):
+        queue = started if queue is None else queue
+        if window and len(queue) >= window:
+            queue.pop(0).wait_send()
         copy.start()
-        started.append(copy)
+        queue.append(copy)
 
     def node_copy(p):
         to = flip(n, order[p])
         return remote(outgoing.at[to], arrived.at[p, c, y], s_node.at[p], r_node.at[p], dev(to, y, c))
 
-    for p in reversed(range(nodes)):
+    def straight_copy(p, d):
+        to = flip(n, order[p])
+        return remote(
+            outgoing.at[to], arrived.at[p, c, y], s_chip.at[d - 1, p], r_chip.at[d - 1, p],
+            dev(to, chip_at(d), c),
+        )
+
+    def send_out(p):
         if p != p_own:
-            go(node_copy(p))
+            go(node_copy(p), node_queue, node_window)
+        if p in early:
+            for d in range(1, chips):
+                go(straight_copy(p, d))
+
+    ahead = min(node_window + 1, nodes) if node_window else nodes
+    for p in range(ahead):
+        send_out(p)
 
     def core_copy(p):
         slab = arrived.at[p, c, y]
@@ -131,8 +146,9 @@
     def spread(p):
         if p != p_own:
             node_copy(p).wait_recv()
-        for d in range(1, chips):
-            go(chip_copy(p, d))
+        if p not in early:
+            for d in range(1, chips):
+                go(chip_copy(p, d), chip_queue, chip_window)
         go(core_copy(p))
 
     def forward(p):
@@ -167,8 +183,9 @@
             partial[lo:hi, :, :, :, cols] = value.astype(jnp.bfloat16).reshape(
                 hi - lo, 2, chips, slots, step
             )
-        for p in range(lo, hi):
-            go(core_copy2(p))
+        for p in way_back:
+            if lo <= p < hi:
+                go(core_copy2(p))
 
     def chip_copy2(p, d):
         return remote(
@@ -182,7 +199,7 @@
             other = chip_at(d)
             both = partial[p, c, other].astype(jnp.float32) + from_core[p, other].astype(jnp.float32)
             chip_sum[p, d - 1] = both.astype(jnp.bfloat16)
-            go(chip_copy2(p, d))
+            go(chip_copy2(p, d), chip_queue2, chip_window2)
 
     def node_copy2(p):
         return remote(
@@ -198,48 +215,56 @@
             back[n] = total.astype(jnp.bfloat16)
         else:
             expert_out[p] = total.astype(jnp.bfloat16)
-            go(node_copy2(p))
-
-    lag = 2
+            go(node_copy2(p), node_queue2, node_window2)
+
     for p in range(nodes + lag):
         if p < nodes:
             spread(p)
+            if p + ahead < nodes:
+                send_out(p + ahead)
         if p >= lag:
             forward(p - lag)
     bounds = [(i * nodes // groups, (i + 1) * nodes // groups) for i in range(groups)]
     for lo, hi in bounds:
         compute(lo, hi)
-        for p in range(lo, hi):
-            to_chips(p)
-    for p in range(nodes):
-        to_nodes(p)
+    for i in range(nodes + lag2):
+        if i < nodes:
+            to_chips(way_back[i])
+        if i >= lag2:
+            to_nodes(way_back[i - lag2])
     for p in range(nodes):
         if p != p_own:
             src = flip(n, order[p])
             remote(
                 expert_out.at[p], back.at[src], s_node2.at[p], r_node2.at[p], dev(src, y, c)
             ).wait_recv()
+    over_places = (((0,), (0,)), ((), ()))
     for cols in columns:
         rows_back = back[:, :, cols].reshape(places, step)
-        mixed = jnp.dot(weight_hi, rows_back, preferred_element_type=jnp.float32)
-        mixed += jnp.dot(weight_lo, rows_back, preferred_element_type=jnp.float32)
+        mixed = sum(
+            lax.dot_general(part, rows_back, over_places, preferred_element_type=jnp.float32)
+            for part in (weight_hi, weight_lo)
+        )
         out_ref[:, cols] = mixed.astype(jnp.bfloat16)
-    for copy in started:
+    for copy in started + node_queue + chip_queue + chip_queue2 + node_queue2:
         copy.wait_send()
 
 
 def body(nodes, chips, tokens, expert_ids, combine_weights, w_gate, w_up, w_down):
     rows, width = tokens.shape
     units = w_gate.shape[2]
-    order = sorted(range(nodes), key=lambda k: (k.bit_count(), k))
-    groups = 2
+    order = list(range(nodes))
+    early = []
+    way_back = list(reversed(range(nodes)))
+    groups = 1
+    windows = (0, 0, 0, 0, 2, 3)
     slab = (CAP, width)
     bf = jnp.bfloat16
     sems = pltpu.SemaphoreType.DMA
     vmem = pl.BlockSpec(memory_space=pltpu.VMEM)
     hbm = pl.BlockSpec(memory_space=pl.ANY)
     return pl.pallas_call(
-        functools.partial(kernel, nodes, chips, order, groups),
+        functools.partial(kernel, nodes, chips, order, early, way_back, groups, windows),
         out_shape=jax.ShapeDtypeStruct((rows, width), bf),
         in_specs=[vmem, vmem, vmem, hbm, hbm, hbm],
         out_specs=vmem,
@@ -269,7 +294,7 @@
             collective_id=0, has_side_effects=True, vmem_limit_bytes=56 * 1024 * 1024
         ),
         name="routed_experts",
-    )(tokens, expert_ids, combine_weights, w_gate, w_up, w_down)
+    )(tokens, expert_ids.T, combine_weights.T, w_gate, w_up, w_down)
 
 
 def solution(mesh):

time: 52.4 us -> 43.4 us (0.83)
  Pallas kernels: 47.8 us -> 41.6 us
  local copies, waits for them, and re-layouts: 4.34 us -> 1.64 us
    pallas_call x1, Pallas kernels: 47.8 us -> 41.6 us  [body(): pl.pallas_call(functools.partial(kernel, nodes, chips, order, early, way_...]
    unnamed x3 -> x1, local copies, waits for them, and re-layouts: 4.34 us -> 1.64 us
where the time goes in v2:
time: 43.4 us; the launch traced here: 43.3 us
  Pallas kernels  41.6 us (96%)
  local copies, waits for them, and re-layouts  1.64 us (4%)
    pallas_call x1, Pallas kernels, body(): pl.pallas_call(functools.partial(kernel, nodes, chips, order, early, way_...  41.6 us
    unnamed x1, local copies, waits for them, and re-layouts  1.64 us

profile of v2, /device:TPU:0, one launch (start us, length us, event | category | flops | bytes accessed | tf_op | source)
XLA Modules:
  0.0 43.3 jit_solution(5493841616426053913)
XLA Ops:
  0.0 41.6 %routed_experts.1 = bf16[16,7168]{1,0:T(8,128)(2,1)} custom-call(bf16[16,7168]{1,0:T(8,128)(2,1)} %tok_ref.1, s32[2,16]{1,0:T(2,128)} %bitcast.2, f32[2,16]{1,0:T(2,128)} %bitcast.3, bf16[1,7168,256]{2,1,0:T(8,128)(2,1)} %gate_hbm.1, bf16[1,7168,256]{2,1,0:T(8,128)(2,1)} %up_hbm.1, bf16[1,256,7168]{2,1,0:T(8,128)(2,1)} %down_hbm.1), custom_call_target="tpu_custom_call" | custom-call | tf_op jit(solution)/shard_map/routed_experts/pallas_call | solution.py:266
  41.6 1.6 %copy.8 = bf16[16,7168]{1,0:T(8,128)(2,1)} copy(bf16[16,7168]{1,0:T(8,128)(2,1)} %routed_experts.1) | data formatting | bytes 458752

commit v3 on v2

--- a/solution.py
+++ b/solution.py
@@ -255,7 +255,8 @@
     units = w_gate.shape[2]
     order = list(range(nodes))
     early = []
-    way_back = list(reversed(range(nodes)))
+    half = nodes // 2
+    way_back = [p - i for i in range(half) for p in (nodes - 1, half - 1)]
     groups = 1
     windows = (0, 0, 0, 0, 2, 3)
     slab = (CAP, width)

time: 43.4 us -> 43.1 us (level)
  no operation moved by 1% of the time
where the time goes in v3:
time: 43.1 us; the launch traced here: 43 us
  Pallas kernels  41.3 us (96%)
  local copies, waits for them, and re-layouts  1.64 us (4%)
    pallas_call x1, Pallas kernels, body(): pl.pallas_call(functools.partial(kernel, nodes, chips, order, early, way_...  41.3 us
    unnamed x1, local copies, waits for them, and re-layouts  1.64 us

profile of v3, /device:TPU:0, one launch (start us, length us, event | category | flops | bytes accessed | tf_op | source)
XLA Modules:
  0.0 43.0 jit_solution(11795331805696449634)
XLA Ops:
  0.0 41.3 %routed_experts.1 = bf16[16,7168]{1,0:T(8,128)(2,1)} custom-call(bf16[16,7168]{1,0:T(8,128)(2,1)} %tok_ref.1, s32[2,16]{1,0:T(2,128)} %bitcast.2, f32[2,16]{1,0:T(2,128)} %bitcast.3, bf16[1,7168,256]{2,1,0:T(8,128)(2,1)} %gate_hbm.1, bf16[1,7168,256]{2,1,0:T(8,128)(2,1)} %up_hbm.1, bf16[1,256,7168]{2,1,0:T(8,128)(2,1)} %down_hbm.1), custom_call_target="tpu_custom_call" | custom-call | tf_op jit(solution)/shard_map/routed_experts/pallas_call | solution.py:267
  41.3 1.6 %copy.8 = bf16[16,7168]{1,0:T(8,128)(2,1)} copy(bf16[16,7168]{1,0:T(8,128)(2,1)} %routed_experts.1) | data formatting | bytes 458752
